TPU v7x, 32 devices: a whole 2x2x4 slice. The times are simulated.
32 devices in a mesh: blk: 8 (over y, x, core), off: 4 (over z).
Axes of the slice: x: 2, y: 2, z: 4, core: 2. Of those that a mesh axis runs over, the one named last changes fastest.
Arguments:
- coefficients: bfloat16 [128, 32, 128], P('blk', 'off'), may hold values from -12 to 12
Outputs:
- smoothed: float32 [128, 32, 128], P(('blk', 'off'))
- log_degree: float32 [128], P(('blk', 'off'))
All inputs are finite; a program needn't handle non-finite values.
Results may differ from a plain program's by a relative error of at most 0.005.
Values may be sent and summed in bfloat16 or wider, within the bound.
No kernel may reach another device: no remote copies, remote signals or barrier semaphores. Data moves between devices by JAX's collectives and lax.ppermute only.
A program may use at most 64 MiB of HBM per device.

v0:
```python
import math
import jax
import jax.numpy as jnp
from jax import lax
from jax.sharding import PartitionSpec as P

epsilon = 1e-06
concentration = 40.0


def shifted(array, axis, by):
    count = lax.axis_size(axis)
    return lax.ppermute(array, axis, [(i, (i + by) % count) for i in range(count)])


def angle_tables(angular):
    half_width = angular // 2
    frequency = jnp.arange(half_width, dtype=jnp.int32)
    shifts = jnp.arange(angular, dtype=jnp.int32)
    product = frequency[:, None] * shifts[None, :] % angular
    phase = product.astype(jnp.float32) * (2.0 * math.pi / angular)
    forward = jnp.concatenate([jnp.cos(phase), -jnp.sin(phase)], axis=0)
    return (forward, forward.T)


def inverse_norms(block_values):
    values = block_values.astype(jnp.float32)
    return lax.rsqrt(jnp.sum(values * values, axis=(1, 2)) + epsilon)


def tile_terms(own_block, own_inverse, other_block, offset, forward, backward):
    row_count = own_block.shape[0]
    half_width = own_block.shape[2] // 2
    highest = lax.Precision.HIGHEST
    other_inverse = inverse_norms(other_block)
    swapped = jnp.concatenate(
        [other_block[:, :, half_width:], other_block[:, :, :half_width]], axis=2
    )
    direct = jnp.einsum("irc,jrc->ijc", own_block, other_block, preferred_element_type=jnp.float32)
    mixed_terms = jnp.einsum("irc,jrc->ijc", own_block, swapped, preferred_element_type=jnp.float32)
    real_part = direct[:, :, :half_width] + direct[:, :, half_width:]
    imag_part = mixed_terms[:, :, half_width:] - mixed_terms[:, :, :half_width]
    cross_spectrum = jnp.concatenate([real_part, imag_part], axis=2).reshape(
        row_count * row_count, -1
    )
    correlation = jnp.dot(
        cross_spectrum, forward, precision=highest, preferred_element_type=jnp.float32
    )
    correlation = correlation.reshape(row_count, row_count, -1)
    cosine = correlation * own_inverse[:, None, None] * other_inverse[None, :, None]
    same_image = jnp.arange(row_count)[:, None] == jnp.arange(row_count)[None, :]
    keep_mask = jnp.where(jnp.logical_and(offset == 0, same_image), 0.0, 1.0).astype(jnp.float32)
    weights = jnp.exp(concentration * cosine) * keep_mask[:, :, None]
    spectral = jnp.dot(
        weights.reshape(row_count * row_count, -1),
        backward,
        precision=highest,
        preferred_element_type=jnp.float32,
    ).reshape(row_count, row_count, -1)
    degree = jnp.sum(spectral[:, :, 0], axis=1)
    rounded = spectral.astype(jnp.bfloat16)
    weight_real = jnp.concatenate([rounded[:, :, :half_width], rounded[:, :, :half_width]], axis=2)
    weight_imag = jnp.concatenate([-rounded[:, :, half_width:], rounded[:, :, half_width:]], axis=2)
    filtered = jnp.einsum(
        "ijc,jrc->irc", weight_real, other_block, preferred_element_type=jnp.float32
    )
    filtered = filtered + jnp.einsum(
        "ijc,jrc->irc", weight_imag, swapped, preferred_element_type=jnp.float32
    )
    return (filtered, degree)


def body(coefficients):
    own_block = lax.all_gather(coefficients, "off", axis=1, tiled=True)
    own_inverse = inverse_norms(own_block)
    row_count, radial, angular = own_block.shape
    forward, backward = angle_tables(angular)
    ranges = lax.axis_size("off")
    per_range = min(8, lax.axis_size("blk") // ranges)
    range_index = lax.axis_index("off")
    range_base = range_index * per_range
    packet = own_block
    packet = shifted(packet, "blk", -(per_range // 2))
    for bit_number in range(ranges.bit_length() - 1):
        moved_packet = shifted(packet, "blk", -(per_range << bit_number))
        chosen = range_index // (1 << bit_number) % 2 == 1
        packet = jnp.where(chosen, moved_packet, packet)
    empty_sum = jnp.zeros((row_count, radial, angular), jnp.float32)
    empty_degree = jnp.zeros((row_count,), jnp.float32)
    centre = range_base + per_range // 2
    lower_block = shifted(packet, "blk", 1)

    def advance_both(step, loop_state):
        filtered, degree, upper_block, lower_part = loop_state
        upper_terms = tile_terms(
            own_block, own_inverse, upper_block, centre + step, forward, backward
        )
        lower_terms = tile_terms(
            own_block, own_inverse, lower_part, centre - 1 - step, forward, backward
        )
        upper_block = shifted(upper_block, "blk", -1)
        lower_part = shifted(lower_part, "blk", 1)
        return (
            filtered + upper_terms[0] + lower_terms[0],
            degree + upper_terms[1] + lower_terms[1],
            upper_block,
            lower_part,
        )

    last_step = per_range // 2 - 1
    filtered, degree, upper_block, lower_block = lax.fori_loop(
        0, last_step, advance_both, (empty_sum, empty_degree, packet, lower_block)
    )
    upper_terms = tile_terms(
        own_block, own_inverse, upper_block, centre + last_step, forward, backward
    )
    lower_terms = tile_terms(
        own_block, own_inverse, lower_block, centre - 1 - last_step, forward, backward
    )
    filtered = filtered + upper_terms[0] + lower_terms[0]
    degree = degree + upper_terms[1] + lower_terms[1]
    totals = (
        lax.psum_scatter(filtered, "off", scatter_dimension=0, tiled=True),
        lax.psum_scatter(degree, "off", scatter_dimension=0, tiled=True),
    )
    smoothed = totals[0] / totals[1][:, None, None]
    return (smoothed, jnp.log(totals[1]))


def solution(mesh):
    return jax.shard_map(
        body,
        mesh=mesh,
        in_specs=(P("blk", "off", None),),
        out_specs=(P(("blk", "off"), None, None), P(("blk", "off"))),
        check_vma=False,
    )
```

profile of v0, /device:TPU:0, one launch (start us, length us, event | category | flops | bytes accessed | tf_op | source)
XLA Modules:
  0.0 91.2 jit_solution(6162711789580707457)
XLA Ops:
  7.2 1.0 %copy.17 = bf16[16,8,128]{0,1,2:T(8,128)(2,1)S(1)} copy(bf16[16,8,128]{2,1,0:T(8,128)(2,1)} %param.1) | data formatting | bytes 65536 | tf_op args[0]
  8.2 23.4 %all_gather.3 = bf16[16,32,128]{0,1,2:T(8,128)(2,1)S(1)} all-gather(bf16[16,8,128]{0,1,2:T(8,128)(2,1)S(1)} %copy.17), channel_id=1, replica_groups=mesh['blk'=8,'off'=4] {'off'}, dimensions={1}, use_global_device_ids=true | all-gather | bytes 163840 | tf_op jit(solution)/shard_map/all_gather | solution.py:74
  31.6 1.2 %copy.18 = bf16[16,32,128]{2,1,0:T(8,128)(2,1)S(1)} copy(bf16[16,32,128]{0,1,2:T(8,128)(2,1)S(1)} %all_gather.3) | data formatting | bytes 262144 | tf_op jit(solution)/shard_map/all_gather | solution.py:74
  32.8 1.2 %collective-permute-start = (bf16[16,32,128]{2,1,0:T(8,128)(2,1)S(1)}, bf16[16,32,128]{2,1,0:T(8,128)(2,1)S(1)}, u32[]{:S(2)}, u32[]{:S(2)}) collective-permute-start(bf16[16,32,128]{2,1,0:T(8,128)(2,1)S(1)} %copy.18), channel_id=1, source_target_pairs={{0,28},{4,0},{8,4},{12,8},{16,12},{20,16},{24,20},{28,24},{1,29},{... | collective-permute-start | bytes 393224 | tf_op jit(solution)/shard_map/ppermute | solution.py:13
  34.0 0.6 multiply_reduce_fusion
  34.5 2.0 %collective-permute-done = bf16[16,32,128]{2,1,0:T(8,128)(2,1)S(1)} collective-permute-done((bf16[16,32,128]{2,1,0:T(8,128)(2,1)S(1)}, bf16[16,32,128]{2,1,0:T(8,128)(2,1)S(1)}, u32[]{:S(2)}, u32[]{:S(2)}) %collective-permute-start) | collective-permute-done | bytes 131104 | tf_op jit(solution)/shard_map/ppermute | solution.py:13
  36.5 1.3 %collective-permute-start.1 = (bf16[16,32,128]{2,1,0:T(8,128)(2,1)S(1)}, bf16[16,32,128]{2,1,0:T(8,128)(2,1)S(1)}, u32[]{:S(2)}, u32[]{:S(2)}) collective-permute-start(bf16[16,32,128]{2,1,0:T(8,128)(2,1)S(1)} %collective-permute-done), channel_id=1, source_target_pairs={{0,24},{4,28},{8,0},{12,4},{16,8},{20,12},{24,16},{28,20},{1,25},{... | collective-permute-start | bytes 393224 | tf_op jit(solution)/shard_map/ppermute | solution.py:13
  37.9 4.7 %collective-permute-done.1 = bf16[16,32,128]{2,1,0:T(8,128)(2,1)S(1)} collective-permute-done((bf16[16,32,128]{2,1,0:T(8,128)(2,1)S(1)}, bf16[16,32,128]{2,1,0:T(8,128)(2,1)S(1)}, u32[]{:S(2)}, u32[]{:S(2)}) %collective-permute-start.1) | collective-permute-done | bytes 131104 | tf_op jit(solution)/shard_map/ppermute | solution.py:13
  42.5 0.3 collective-permute-start.2
  42.9 0.1 sine_negate_fusion
  43.0 4.8 %collective-permute-done.2 = bf16[16,32,128]{2,1,0:T(8,128)(2,1)S(1)} collective-permute-done((bf16[16,32,128]{2,1,0:T(8,128)(2,1)S(1)}, bf16[16,32,128]{2,1,0:T(8,128)(2,1)S(1)}, u32[]{:S(2)}, u32[]{:S(2)}) %collective-permute-start.2) | collective-permute-done | bytes 131104 | tf_op jit(solution)/shard_map/ppermute | solution.py:13
  47.8 0.2 multiply_reduce_fusion.2
  48.0 0.2 collective-permute-start.3
  48.3 0.4 copy.23
  48.9 0.4 copy.20
  49.3 0.4 convolution_bitcast_fusion.2
  49.8 0.3 copy.22
  50.1 0.4 convolution_bitcast_fusion.3
  50.6 0.3 copy.21
  50.9 0.3 fusion.5
  51.2 0.3 fusion.39
  51.7 0.4 copy.26
  52.1 1.4 %fusion.40 = f32[128,32,16]{1,2,0:T(8,128)} fusion(bf16[16,16,128]{1,0,2:T(8,128)(2,1)S(1)} %copy.26, bf16[16,32,128]{1,0,2:T(8,128)(2,1)S(1)} %copy.20), kind=kOutput, calls=%fused_computation.77 | convolution fusion | flops 2097152 | bytes 458752 | tf_op jit(solution)/shard_map/ijc,jrc->irc/dot_general | solution.py:67
  53.6 1.2 %copy.24 = bf16[16,16,128]{1,0,2:T(8,128)(2,1)} copy(bf16[16,16,128]{2,1,0:T(8,128)(2,1)S(1)} %pad_maximum_fusion.2) | data formatting | bytes 131072 | tf_op jit(solution)/shard_map/concatenate | solution.py:62
  55.1 0.4 copy.28
  55.5 0.4 convolution_bitcast_fusion
  56.0 0.3 copy.30
  56.3 0.4 copy.31
  56.7 0.4 convolution_bitcast_fusion.1
  57.2 0.3 copy.29
  57.5 0.2 multiply_reduce_fusion.1
  57.7 0.3 fusion.9
  58.0 0.3 fusion.38
  58.5 0.4 copy.34
  58.9 0.4 fusion.41
  59.4 0.4 copy.32
  59.9 0.4 convolution_add_fusion
  60.3 0.8 copy-done
  61.1 0.1 copy-done.1
  61.2 0.4 fusion.1
  61.6 1.1 %copy.35 = f32[16,32,128]{2,1,0:T(8,128)} copy(f32[16,32,128]{1,0,2:T(8,128)S(1)} %fusion.1) | data formatting | bytes 524288 | tf_op jit(solution)/shard_map/add | solution.py:120
  62.8 0.6 dynamic-slice
  64.0 0.2 slice_reduce_fusion.1
  64.2 0.2 slice_reduce_fusion
  64.4 10.6 %all-reduce = f32[16]{0:T(128)S(1)} all-reduce(f32[16]{0:T(128)S(1)} %add.84), channel_id=3, replica_groups=mesh['blk'=8,'off'=4] {'off'}, use_global_device_ids=true, to_apply=%region_6.7.clone | all-reduce | flops 16 | bytes 128
  75.0 0.6 fusion.33
  75.6 7.2 %reduce-scatter.2.cloned.1.call-done = f32[4,32,128]{2,1,0:T(8,128)} async-done(((f32[16,32,128]{2,1,0:T(8,128)}), f32[4,32,128]{2,1,0:T(8,128)}) %reduce-scatter.2.cloned.1.call-update) | async-done | bytes 65552 | tf_op jit(solution)/shard_map/reduce_scatter | solution.py:123
  82.8 1.5 %broadcast_divide_fusion = f32[4,32,128]{2,1,0:T(8,128)} fusion(f32[4,32,128]{2,1,0:T(8,128)} %reduce-scatter.2.cloned.1.call-done, f32[4]{0:T(128)S(1)} %get-tuple-element.5), kind=kLoop, calls=%fused_computation.48 | loop fusion | flops 16384 | bytes 131088 | tf_op jit(solution)/shard_map/div | solution.py:126
  (28 shorter events, 1.4 us)
Async XLA Ops:
  7.2 75.7 %reduce-scatter.2.cloned.1.call-start = ((), (), s32[]{:S(2)}) async-start(), calls=%async_computation.1 | async-start | bytes 327680 | tf_op jit(solution)/shard_map/reduce_scatter | solution.py:123
  32.8 3.7 %collective-permute-start = (bf16[16,32,128]{2,1,0:T(8,128)(2,1)S(1)}, bf16[16,32,128]{2,1,0:T(8,128)(2,1)S(1)}, u32[]{:S(2)}, u32[]{:S(2)}) collective-permute-start(bf16[16,32,128]{2,1,0:T(8,128)(2,1)S(1)} %copy.18), channel_id=1, source_target_pairs={{0,28},{4,0},{8,4},{12,8},{16,12},{20,16},{24,20},{28,24},{1,29},{... | collective-permute-start | bytes 393224 | tf_op jit(solution)/shard_map/ppermute | solution.py:13
  36.5 6.0 %collective-permute-start.1 = (bf16[16,32,128]{2,1,0:T(8,128)(2,1)S(1)}, bf16[16,32,128]{2,1,0:T(8,128)(2,1)S(1)}, u32[]{:S(2)}, u32[]{:S(2)}) collective-permute-start(bf16[16,32,128]{2,1,0:T(8,128)(2,1)S(1)} %collective-permute-done), channel_id=1, source_target_pairs={{0,24},{4,28},{8,0},{12,4},{16,8},{20,12},{24,16},{28,20},{1,25},{... | collective-permute-start | bytes 393224 | tf_op jit(solution)/shard_map/ppermute | solution.py:13
  42.5 5.2 %collective-permute-start.2 = (bf16[16,32,128]{2,1,0:T(8,128)(2,1)S(1)}, bf16[16,32,128]{2,1,0:T(8,128)(2,1)S(1)}, u32[]{:S(2)}, u32[]{:S(2)}) collective-permute-start(bf16[16,32,128]{2,1,0:T(8,128)(2,1)S(1)} %broadcast_select_fusion), channel_id=1, source_target_pairs={{0,16},{4,20},{8,24},{12,28},{16,0},{20,4},{24,8},{28,12},{1,17},{... | collective-permute-start | bytes 393224 | tf_op jit(solution)/shard_map/ppermute | solution.py:13
  48.0 6.8 %collective-permute-start.3 = (bf16[16,32,128]{2,1,0:T(8,128)(2,1)S(1)}, bf16[16,32,128]{2,1,0:T(8,128)(2,1)S(1)}, u32[]{:S(2)}, u32[]{:S(2)}) collective-permute-start(bf16[16,32,128]{2,1,0:T(8,128)(2,1)S(1)} %get-tuple-element.7), channel_id=1, source_target_pairs={{0,4},{4,8},{8,12},{12,16},{16,20},{20,24},{24,28},{28,0},{1,5},{5... | collective-permute-start | bytes 393224 | tf_op jit(solution)/shard_map/ppermute | solution.py:13
  59.9 1.2 %copy-start = (f32[128,32,16]{1,2,0:T(8,128)S(1)}, f32[128,32,16]{1,2,0:T(8,128)}, u32[]{:S(2)}) copy-start(f32[128,32,16]{1,2,0:T(8,128)} %fusion.40) | copy-start | bytes 786436
  59.9 1.3 %copy-start.1 = (bf16[16,16,128]{1,0,2:T(8,128)(2,1)S(1)}, bf16[16,16,128]{1,0,2:T(8,128)(2,1)}, u32[]{:S(2)}) copy-start(bf16[16,16,128]{1,0,2:T(8,128)(2,1)} %copy.24) | copy-start | bytes 196612
  61.6 1.2 %copy-start.2 = (u32[32]{0:T(128)S(1)}, u32[32]{0:T(128)}, u32[]{:S(2)}) copy-start(u32[32]{0:T(128)} %constant.70) | copy-start | bytes 388
Sparse Core Ops, SparseCore 0:
  62.9 19.8 reduce-scatter.1
where the time goes:
time: 91.5 us; the launch traced here: 91.2 us
  blocking collectives  34 us (37%)
  waiting for transfers between devices  18.7 us (20%)
  between operations  15 us (16%)
  local copies, waits for them, and re-layouts  10.9 us (12%)
  matrix products  5.46 us (6%)
  other arithmetic  4.18 us (5%)
  starting transfers between devices  3.05 us (3%)
    all_gather x1, blocking collectives, body(): own_block = lax.all_gather(coefficients, 'off', axis=1, tiled=True)  23.4 us
    ppermute x4, waiting for transfers between devices, shifted(): lax.ppermute(array, axis, [(i, (i + by) % count) for i in range(count)])  11.4 us
    unnamed x1, blocking collectives  10.6 us
    reduce_scatter x1, waiting for transfers between devices, body(): lax.psum_scatter(filtered, 'off', scatter_dimension=0, tiled=True)  7.22 us
    ppermute x4, starting transfers between devices, shifted(): lax.ppermute(array, axis, [(i, (i + by) % count) for i in range(count)])  3.02 us
    unnamed x8, local copies, waits for them, and re-layouts  2.54 us
  transfers between devices with their start and end apart: 5, of which 4 were waited for; matrix products, arithmetic and copies ran while one was open for 10% of the time, Pallas kernels for 0%

commit v1 on v0

--- a/solution.py
+++ b/solution.py
@@ -6,6 +6,19 @@
 
 epsilon = 1e-06
 concentration = 40.0
+
+
+def gather_around(x, axis, dim):
+    ways = lax.axis_size(axis)
+    up = [(d, (d + 1) % ways) for d in range(ways)]
+    down = [(d, (d - 1) % ways) for d in range(ways)]
+    earlier, later = ([x], [x])
+    for _ in range(ways // 2):
+        earlier.append(lax.ppermute(earlier[-1], axis, up))
+    for _ in range((ways - 1) // 2):
+        later.append(lax.ppermute(later[-1], axis, down))
+    line = jnp.concatenate([*earlier[::-1], *later[1:]], axis=dim)
+    return jnp.roll(line, (lax.axis_index(axis) - ways // 2) * x.shape[dim], axis=dim)
 
 
 def shifted(array, axis, by):
@@ -71,7 +84,7 @@
 
 
 def body(coefficients):
-    own_block = lax.all_gather(coefficients, "off", axis=1, tiled=True)
+    own_block = gather_around(coefficients, "off", 1)
     own_inverse = inverse_norms(own_block)
     row_count, radial, angular = own_block.shape
     forward, backward = angle_tables(angular)

time: 91.5 us -> 134 us (1.46)
  waiting for transfers between devices: 18.7 us -> 73.2 us
  blocking collectives: 34 us -> 10.1 us
  starting transfers between devices: 3.05 us -> 8.82 us
  local copies, waits for them, and re-layouts: 10.9 us -> 16 us
  other arithmetic: 4.18 us -> 5.66 us
    ppermute x0 -> x3, waiting for transfers between devices: none -> 34.4 us  [the longest x2 24.4 us: gather_around(): earlier.append(lax.ppermute(earlier[-1], axis, up))]
    all_gather x1 -> x0, blocking collectives: 23.4 us -> none  [body(): own_block = lax.all_gather(coefficients, 'off', axis=1, tiled=True)]
    ppermute x4, waiting for transfers between devices: 11.4 us -> 31.9 us  [shifted(): lax.ppermute(array, axis, [(i, (i + by) % count) for i in range(count)])]
    ppermute x0 -> x3, starting transfers between devices: none -> 5.17 us  [the longest x2 3.08 us: gather_around(): earlier.append(lax.ppermute(earlier[-1], axis, up))]
    concatenate x2 -> x1, local copies, waits for them, and re-layouts: 0.86 us -> 5.3 us  [gather_around(): jnp.roll(line, (lax.axis_index(axis) - ways // 2) * x.shape[dim], axis=dim)]
  transfers between devices with their start and end apart: 5 -> 8, of which waited for: 4 -> 8; matrix products, arithmetic and copies ran while one was open for 10% -> 8% of each run, Pallas kernels for 0% -> 0%
where the time goes in v1:
time: 134 us
  waiting for transfers between devices  73.2 us (55%)
  local copies, waits for them, and re-layouts  16 us (12%)
  between operations  14.9 us (11%)
  blocking collectives  10.1 us (8%)
  starting transfers between devices  8.82 us (7%)
  other arithmetic  5.66 us (4%)
  matrix products  5.34 us (4%)
    ppermute x4, waiting for transfers between devices, shifted(): lax.ppermute(array, axis, [(i, (i + by) % count) for i in range(count)])  31.9 us
    ppermute x2, waiting for transfers between devices, gather_around(): earlier.append(lax.ppermute(earlier[-1], axis, up))  24.4 us
    unnamed x1, blocking collectives  10.1 us
    ppermute x1, waiting for transfers between devices, gather_around(): later.append(lax.ppermute(later[-1], axis, down))  10 us
    reduce_scatter x1, waiting for transfers between devices, body(): lax.psum_scatter(filtered, 'off', scatter_dimension=0, tiled=True)  6.85 us
    concatenate x1, local copies, waits for them, and re-layouts, gather_around(): jnp.roll(line, (lax.axis_index(axis) - ways // 2) * x.shape[dim], axis=dim)  5.3 us
    ppermute x4, starting transfers between devices, shifted(): lax.ppermute(array, axis, [(i, (i + by) % count) for i in range(count)])  3.62 us
    unnamed x8, local copies, waits for them, and re-layouts  3.35 us
  transfers between devices with their start and end apart: 8, of which 8 were waited for; matrix products, arithmetic and copies ran while one was open for 8% of the time, Pallas kernels for 0%

profile of v1, /device:TPU:0, one launch (start us, length us, event | category | flops | bytes accessed | tf_op | source)
XLA Modules:
  0.0 134.0 jit_solution(9230879188101240140)
XLA Ops:
  7.2 1.2 copy.33
  8.4 3.1 %collective-permute-start = (bf16[16,8,128]{1,0,2:T(8,128)(2,1)S(1)}, bf16[16,8,128]{1,0,2:T(8,128)(2,1)S(1)}, u32[]{:S(2)}, u32[]{:S(2)}) collective-permute-start(bf16[16,8,128]{1,0,2:T(8,128)(2,1)S(1)} %copy.33), channel_id=1, source_target_pairs={{0,1},{1,2},{2,3},{3,0},{4,5},{5,6},{6,7},{7,4},{8,9},{9,10},{10,1... | collective-permute-start | bytes 98312 | tf_op jit(solution)/shard_map/ppermute | solution.py:17
  11.5 2.1 %collective-permute-start.2 = (bf16[16,8,128]{1,0,2:T(8,128)(2,1)S(1)}, bf16[16,8,128]{1,0,2:T(8,128)(2,1)S(1)}, u32[]{:S(2)}, u32[]{:S(2)}) collective-permute-start(bf16[16,8,128]{1,0,2:T(8,128)(2,1)S(1)} %copy.33), channel_id=1, source_target_pairs={{0,3},{1,0},{2,1},{3,2},{4,7},{5,4},{6,5},{7,6},{8,11},{9,8},{10,9... | collective-permute-start | bytes 98312 | tf_op jit(solution)/shard_map/ppermute | solution.py:19
  13.6 12.7 %collective-permute-done = bf16[16,8,128]{1,0,2:T(8,128)(2,1)S(1)} collective-permute-done((bf16[16,8,128]{1,0,2:T(8,128)(2,1)S(1)}, bf16[16,8,128]{1,0,2:T(8,128)(2,1)S(1)}, u32[]{:S(2)}, u32[]{:S(2)}) %collective-permute-start) | collective-permute-done | bytes 32800 | tf_op jit(solution)/shard_map/ppermute | solution.py:17
  26.3 10.0 %collective-permute-done.2 = bf16[16,8,128]{1,0,2:T(8,128)(2,1)S(1)} collective-permute-done((bf16[16,8,128]{1,0,2:T(8,128)(2,1)S(1)}, bf16[16,8,128]{1,0,2:T(8,128)(2,1)S(1)}, u32[]{:S(2)}, u32[]{:S(2)}) %collective-permute-start.2) | collective-permute-done | bytes 32800 | tf_op jit(solution)/shard_map/ppermute | solution.py:19
  36.3 11.6 %collective-permute-done.1 = bf16[16,8,128]{1,0,2:T(8,128)(2,1)S(1)} collective-permute-done((bf16[16,8,128]{1,0,2:T(8,128)(2,1)S(1)}, bf16[16,8,128]{1,0,2:T(8,128)(2,1)S(1)}, u32[]{:S(2)}, u32[]{:S(2)}) %collective-permute-start.1) | collective-permute-done | bytes 32800 | tf_op jit(solution)/shard_map/ppermute | solution.py:17
  47.9 5.3 %concatenate.33 = bf16[16,64,128]{1,0,2:T(8,128)(2,1)S(1)} concatenate(bf16[16,8,128]{1,0,2:T(8,128)(2,1)S(1)} %collective-permute-done.1, bf16[16,8,128]{1,0,2:T(8,128)(2,1)S(1)} %collective-permute-done, bf16[16,8,128]{1,0,2:T(8,128)(2,1)S(1)} %copy.33, bf16[16,8,128]{1,0,2:T(8,128)(2,1)S(1)} %collective-permute-done.2, bf16[16,8,128]{1,0,2:T(8,128)(2,1)S(1)} %collective-permute-done.1, ...), dimensions={1} | concatenate | bytes 524288 | tf_op jit(solution)/shard_map/jit(_roll_dynamic)/concatenate | solution.py:21
  53.2 0.4 multiply_reduce_fusion.2
  53.7 6.7 %collective-permute-done.3 = bf16[16,32,128]{1,0,2:T(8,128)(2,1)S(1)} collective-permute-done((bf16[16,32,128]{1,0,2:T(8,128)(2,1)S(1)}, bf16[16,32,128]{1,0,2:T(8,128)(2,1)S(1)}, u32[]{:S(2)}, u32[]{:S(2)}) %collective-permute-start.3) | collective-permute-done | bytes 131104 | tf_op jit(solution)/shard_map/ppermute | solution.py:26
  60.4 2.4 %collective-permute-start.4 = (bf16[16,32,128]{1,0,2:T(8,128)(2,1)S(1)}, bf16[16,32,128]{1,0,2:T(8,128)(2,1)S(1)}, u32[]{:S(2)}, u32[]{:S(2)}) collective-permute-start(bf16[16,32,128]{1,0,2:T(8,128)(2,1)S(1)} %collective-permute-done.3), channel_id=1, source_target_pairs={{0,24},{4,28},{8,0},{12,4},{16,8},{20,12},{24,16},{28,20},{1,25},{... | collective-permute-start | bytes 393224 | tf_op jit(solution)/shard_map/ppermute | solution.py:26
  63.0 11.9 %collective-permute-done.4 = bf16[16,32,128]{1,0,2:T(8,128)(2,1)S(1)} collective-permute-done((bf16[16,32,128]{1,0,2:T(8,128)(2,1)S(1)}, bf16[16,32,128]{1,0,2:T(8,128)(2,1)S(1)}, u32[]{:S(2)}, u32[]{:S(2)}) %collective-permute-start.4) | collective-permute-done | bytes 131104 | tf_op jit(solution)/shard_map/ppermute | solution.py:26
  75.0 1.1 collective-permute-start.5
  76.1 12.9 %collective-permute-done.5 = bf16[16,32,128]{1,0,2:T(8,128)(2,1)S(1)} collective-permute-done((bf16[16,32,128]{1,0,2:T(8,128)(2,1)S(1)}, bf16[16,32,128]{1,0,2:T(8,128)(2,1)S(1)}, u32[]{:S(2)}, u32[]{:S(2)}) %collective-permute-start.5) | collective-permute-done | bytes 131104 | tf_op jit(solution)/shard_map/ppermute | solution.py:26
  89.0 0.4 multiply_reduce_fusion.1
  89.4 0.4 convolution_bitcast_fusion.3
  89.8 0.4 convolution_bitcast_fusion.2
  90.2 0.9 slice_subtract_fusion.1
  91.1 1.3 copy.38
  92.4 0.9 slice_add_fusion.1
  93.2 1.3 copy.37
  94.5 0.3 fusion.5
  94.9 0.3 fusion.45
  95.3 0.4 copy.40
  95.8 1.4 %fusion.11 = f32[128,32,16]{1,2,0:T(8,128)} fusion(bf16[16,16,128]{1,0,2:T(8,128)(2,1)S(1)} %copy.40, bf16[16,32,64]{1,0,2:T(8,128)(2,1)S(1)} %get-tuple-element.11, bf16[16,32,64]{1,0,2:T(8,128)(2,1)S(1)} %get-tuple-element.10), kind=kOutput, calls=%fused_computation.30 | convolution fusion | flops 2359296 | bytes 458752 | tf_op jit(solution)/shard_map/ijc,jrc->irc/dot_general | solution.py:80
  97.3 1.2 copy.39
  98.4 0.4 collective-permute-done.6
  98.9 0.4 convolution_bitcast_fusion
  99.4 0.3 copy.42
  99.6 0.4 convolution_bitcast_fusion.1
  100.1 0.3 copy.41
  100.4 0.3 multiply_reduce_fusion
  100.7 0.3 fusion.9
  101.0 0.3 fusion.44
  101.5 0.4 copy.44
  101.9 0.4 fusion.10
  102.4 0.4 copy.43
  102.9 0.4 convolution_add_fusion
  103.3 0.8 copy-done
  104.2 0.4 fusion.1
  104.6 1.1 copy.45
  105.8 0.6 copy-done.2
  106.4 0.6 dynamic-slice
  107.7 0.2 slice_reduce_fusion.1
  107.9 0.2 slice_reduce_fusion
  108.1 10.1 %all-reduce = f32[16]{0:T(128)S(1)} all-reduce(f32[16]{0:T(128)S(1)} %add.97), channel_id=3, replica_groups=mesh['blk'=8,'off'=4] {'off'}, use_global_device_ids=true, to_apply=%region_6.7.clone | all-reduce | flops 16 | bytes 128
  118.2 0.6 fusion.39
  118.8 6.9 %reduce-scatter.2.cloned.1.call-done = f32[4,32,128]{2,1,0:T(8,128)} async-done(((f32[16,32,128]{2,1,0:T(8,128)}), f32[4,32,128]{2,1,0:T(8,128)}) %reduce-scatter.2.cloned.1.call-update) | async-done | bytes 65552 | tf_op jit(solution)/shard_map/reduce_scatter | solution.py:136
  125.6 1.5 %broadcast_divide_fusion = f32[4,32,128]{2,1,0:T(8,128)} fusion(f32[4,32,128]{2,1,0:T(8,128)} %reduce-scatter.2.cloned.1.call-done, f32[4]{0:T(128)S(1)} %get-tuple-element.5), kind=kLoop, calls=%fused_computation.50 | loop fusion | flops 16384 | bytes 131088 | tf_op jit(solution)/shard_map/div | solution.py:139
  (27 shorter events, 1.3 us)
Async XLA Ops:
  7.2 118.5 %reduce-scatter.2.cloned.1.call-start = ((), (), s32[]{:S(2)}) async-start(), calls=%async_computation.1 | async-start | bytes 327680 | tf_op jit(solution)/shard_map/reduce_scatter | solution.py:136
  8.4 17.9 %collective-permute-start = (bf16[16,8,128]{1,0,2:T(8,128)(2,1)S(1)}, bf16[16,8,128]{1,0,2:T(8,128)(2,1)S(1)}, u32[]{:S(2)}, u32[]{:S(2)}) collective-permute-start(bf16[16,8,128]{1,0,2:T(8,128)(2,1)S(1)} %copy.33), channel_id=1, source_target_pairs={{0,1},{1,2},{2,3},{3,0},{4,5},{5,6},{6,7},{7,4},{8,9},{9,10},{10,1... | collective-permute-start | bytes 98312 | tf_op jit(solution)/shard_map/ppermute | solution.py:17
  11.5 24.8 %collective-permute-start.2 = (bf16[16,8,128]{1,0,2:T(8,128)(2,1)S(1)}, bf16[16,8,128]{1,0,2:T(8,128)(2,1)S(1)}, u32[]{:S(2)}, u32[]{:S(2)}) collective-permute-start(bf16[16,8,128]{1,0,2:T(8,128)(2,1)S(1)} %copy.33), channel_id=1, source_target_pairs={{0,3},{1,0},{2,1},{3,2},{4,7},{5,4},{6,5},{7,6},{8,11},{9,8},{10,9... | collective-permute-start | bytes 98312 | tf_op jit(solution)/shard_map/ppermute | solution.py:19
  26.3 21.6 %collective-permute-start.1 = (bf16[16,8,128]{1,0,2:T(8,128)(2,1)S(1)}, bf16[16,8,128]{1,0,2:T(8,128)(2,1)S(1)}, u32[]{:S(2)}, u32[]{:S(2)}) collective-permute-start(bf16[16,8,128]{1,0,2:T(8,128)(2,1)S(1)} %collective-permute-done), channel_id=1, source_target_pairs={{0,1},{1,2},{2,3},{3,0},{4,5},{5,6},{6,7},{7,4},{8,9},{9,10},{10,1... | collective-permute-start | bytes 98312 | tf_op jit(solution)/shard_map/ppermute | solution.py:17
  53.6 6.8 %collective-permute-start.3 = (bf16[16,32,128]{1,0,2:T(8,128)(2,1)S(1)}, bf16[16,32,128]{1,0,2:T(8,128)(2,1)S(1)}, u32[]{:S(2)}, u32[]{:S(2)}) collective-permute-start(bf16[16,32,128]{1,0,2:T(8,128)(2,1)S(1)} %get-tuple-element.9), channel_id=1, source_target_pairs={{0,28},{4,0},{8,4},{12,8},{16,12},{20,16},{24,20},{28,24},{1,29},{... | collective-permute-start | bytes 393224 | tf_op jit(solution)/shard_map/ppermute | solution.py:26
  60.4 14.5 %collective-permute-start.4 = (bf16[16,32,128]{1,0,2:T(8,128)(2,1)S(1)}, bf16[16,32,128]{1,0,2:T(8,128)(2,1)S(1)}, u32[]{:S(2)}, u32[]{:S(2)}) collective-permute-start(bf16[16,32,128]{1,0,2:T(8,128)(2,1)S(1)} %collective-permute-done.3), channel_id=1, source_target_pairs={{0,24},{4,28},{8,0},{12,4},{16,8},{20,12},{24,16},{28,20},{1,25},{... | collective-permute-start | bytes 393224 | tf_op jit(solution)/shard_map/ppermute | solution.py:26
  75.0 14.0 %collective-permute-start.5 = (bf16[16,32,128]{1,0,2:T(8,128)(2,1)S(1)}, bf16[16,32,128]{1,0,2:T(8,128)(2,1)S(1)}, u32[]{:S(2)}, u32[]{:S(2)}) collective-permute-start(bf16[16,32,128]{1,0,2:T(8,128)(2,1)S(1)} %broadcast_select_fusion), channel_id=1, source_target_pairs={{0,16},{4,20},{8,24},{12,28},{16,0},{20,4},{24,8},{28,12},{1,17},{... | collective-permute-start | bytes 393224 | tf_op jit(solution)/shard_map/ppermute | solution.py:26
  89.3 9.6 %collective-permute-start.6 = (bf16[16,32,128]{1,0,2:T(8,128)(2,1)S(1)}, bf16[16,32,128]{1,0,2:T(8,128)(2,1)S(1)}, u32[]{:S(2)}, u32[]{:S(2)}) collective-permute-start(bf16[16,32,128]{1,0,2:T(8,128)(2,1)S(1)} %get-tuple-element.7), channel_id=1, source_target_pairs={{0,4},{4,8},{8,12},{12,16},{16,20},{20,24},{24,28},{28,0},{1,5},{5... | collective-permute-start | bytes 393224 | tf_op jit(solution)/shard_map/ppermute | solution.py:26
  102.9 1.2 copy-start
  102.9 1.3 %copy-start.1 = (bf16[16,16,128]{1,0,2:T(8,128)(2,1)S(1)}, bf16[16,16,128]{1,0,2:T(8,128)(2,1)}, u32[]{:S(2)}) copy-start(bf16[16,16,128]{1,0,2:T(8,128)(2,1)} %copy.39) | copy-start | bytes 196612
  105.8 0.7 copy-start.2
Sparse Core Ops, SparseCore 0:
  105.9 19.6 reduce-scatter.1
